TPU v7x, 32 devices: a whole 2x2x4 slice. The times are simulated.
32 devices in a mesh: dp: 4 (over y, x), expert: 8 (over z, core).
Axes of the slice: x: 2, y: 2, z: 4, core: 2. Of those that a mesh axis runs over, the one named last changes fastest.
Arguments:
- output_grad: bfloat16 [6144, 2048], P(('dp', 'expert')), may hold values from -3 to 3
- routes: int32 [6144, 2], P(('dp', 'expert')), may hold values from 0 to 7, all different within a row; in each aligned block of 192 rows (0 to 191, 192 to 383, ...) at most 72 rows name the same one
- combine_weights: bfloat16 [6144, 2], P(('dp', 'expert')), may hold values from 0.049804688 to 0.5
- saved_hidden: bfloat16 [18432, 768], P(('dp', 'expert')), may hold values from -0.796875 to 0.796875
- down_weight: bfloat16 [8, 768, 2048], P('expert', 'dp'), may hold values from -0.21875 to 0.21875
Outputs:
- hidden_grad: bfloat16 [18432, 768], P(('dp', 'expert'))
- weight_grad: float32 [8, 768, 2048], P('expert', 'dp')
- route_grad: float32 [6144, 2], P(('dp', 'expert'))
Inputs may be any that keep to these rules, and one draw needn't show every extreme that they name: Each token names 2 different experts; among the 192 rows of one device no expert is named by more than 72 routes.
All inputs are finite; a program needn't handle non-finite values.
Results may differ from a plain program's by a relative error of at most 0.008.
Values may be sent and summed in bfloat16 or wider, within the bound.
A program may use at most 64 MiB of HBM per device.

v0:
```python
import jax
import jax.numpy as jnp
from jax import lax
from jax.sharding import PartitionSpec as P


def route_slots(routes, experts, capacity):
    flat_ids = routes.reshape(-1)
    place = jnp.arange(flat_ids.shape[0], dtype=jnp.int32)
    same = flat_ids[:, None] == flat_ids[None, :]
    rank = jnp.sum((same & (place[None, :] < place[:, None])).astype(jnp.int32), axis=1)
    return flat_ids * capacity + rank


def per_device(output_grad, routes, combine_weights, saved_hidden, down_weight):
    experts = lax.axis_size("expert")
    slot_count = saved_hidden.shape[0]
    capacity = slot_count // experts
    features = output_grad.shape[1]
    route_total = routes.shape[0] * routes.shape[1]
    target = route_slots(routes, experts, capacity)
    source = (
        jnp.full((slot_count,), route_total, jnp.int32)
        .at[target]
        .set(jnp.arange(route_total, dtype=jnp.int32))
    )
    is_live = source < route_total
    safe_index = jnp.where(is_live, source, 0)
    send_rows = jnp.where(
        is_live[:, None], output_grad[safe_index // routes.shape[1]], jnp.zeros((), jnp.bfloat16)
    )
    send_weights = jnp.where(
        is_live, combine_weights.reshape(-1)[safe_index], jnp.zeros((), jnp.bfloat16)
    )
    recv_rows, recv_weights = (
        lax.all_to_all(
            send_rows.reshape(experts, capacity, features),
            "expert",
            split_axis=0,
            concat_axis=0,
            tiled=True,
        ),
        lax.all_to_all(
            send_weights.reshape(experts, capacity),
            "expert",
            split_axis=0,
            concat_axis=0,
            tiled=True,
        ),
    )
    grad_rows = recv_rows.reshape(slot_count, features)
    slot_weights = recv_weights.reshape(slot_count).astype(jnp.float32)
    weighted = (slot_weights[:, None] * grad_rows.astype(jnp.float32)).astype(jnp.bfloat16)
    weight_shard = down_weight[0]
    contract = (((1,), (1,)), ((), ()))
    full_weight = lax.all_gather(weight_shard, "dp", axis=0, tiled=True)
    unscaled = lax.dot_general(grad_rows, full_weight, contract, preferred_element_type=jnp.float32)
    route_terms = jnp.sum(saved_hidden.astype(jnp.float32) * unscaled, axis=1)
    hidden_grad = (slot_weights[:, None] * unscaled).astype(jnp.bfloat16)
    grad_part = lax.psum_scatter(
        lax.dot_general(
            saved_hidden, weighted, (((0,), (0,)), ((), ())), preferred_element_type=jnp.float32
        ).astype(jnp.bfloat16),
        "dp",
        scatter_dimension=0,
        tiled=True,
    ).astype(jnp.float32)
    returned = lax.all_to_all(
        route_terms.reshape(experts, capacity), "expert", split_axis=0, concat_axis=0, tiled=True
    )
    route_grad = returned.reshape(-1)[target].reshape(routes.shape)
    return (hidden_grad, grad_part[None], route_grad)


def solution(mesh):
    return jax.shard_map(
        per_device,
        mesh=mesh,
        in_specs=(
            P(("dp", "expert"), None),
            P(("dp", "expert"), None),
            P(("dp", "expert"), None),
            P(("dp", "expert"), None),
            P("expert", "dp", None),
        ),
        out_specs=(P(("dp", "expert"), None), P("expert", "dp", None), P(("dp", "expert"), None)),
        check_vma=False,
    )
```

profile of v0, /device:TPU:0, one launch (start us, length us, event | category | flops | bytes accessed | tf_op | source)
XLA Modules:
  0.0 155.5 jit_solution(9721528789717610883)
XLA Ops:
  7.2 0.9 copy.21
  8.1 0.7 broadcast_multiply_fusion
  8.7 0.1 eq.15
  8.9 0.2 convert_reduce_fusion
  9.1 0.1 copy.20
  9.2 0.1 mul.37
  9.4 2.9 %scatter_custom_fusion = s32[576]{0:T(1024)S(1)} fusion(s32[384]{0:T(512)S(1)} %fusion.9, s32[384]{0:T(512)S(1)} %iota.10, s32[]{:T(128)} %constant.9.clone.1), kind=kCustom, calls=%fused_computation.32 | custom fusion | bytes 2308 | tf_op jit(solution)/shard_map/scatter | solution.py:25
  12.4 0.8 copy.22
  13.2 0.2 reshape.75
  13.4 3.9 %gather_fusion = bf16[576]{0:T(1024)(128)(2,1)S(1)} fusion(bf16[384]{0:T(512)(128)(2,1)S(1)} %reshape.75, s32[1024]{0:T(1024)S(1)} %pad_clamp_fusion.2), kind=kCustom, calls=%fused_computation | custom fusion | bytes 4608 | tf_op jit(solution)/shard_map/gather | solution.py:33
  17.3 0.7 all_to_all.20
  18.0 6.3 %all-to-all-start = ((bf16[8,1,72]{2,1,0:T(2,128)(2,1)}), bf16[8,1,72]{2,1,0:T(2,128)(2,1)S(1)}, u32[]{:S(2)}, u32[]{:S(2)}) async-start(bf16[8,1,72]{2,1,0:T(2,128)(2,1)} %all_to_all.20), calls=%async_computation | async-start | bytes 8192 | tf_op jit(solution)/shard_map/all_to_all | solution.py:43
  24.4 0.7 all-gather.3.cloned.1.call-update
  25.2 3.4 %gather_fusion.1 = bf16[576,2048]{1,0:T(8,128)(2,1)S(1)} fusion(bf16[192,2048]{1,0:T(8,128)(2,1)S(1)} %copy-done, s32[1024]{0:T(1024)S(1)} %pad_clamp_fusion.1), kind=kCustom, calls=%fused_computation.1 | custom fusion | bytes 4720896 | tf_op jit(solution)/shard_map/gather | solution.py:30
  28.6 1.7 %broadcast_select_fusion = bf16[8,72,2048]{2,1,0:T(8,128)(2,1)} fusion(bf16[8,72,2048]{2,1,0:T(8,128)(2,1)S(1)} %bitcast.15, pred[8,72]{1,0:T(8,128)(4,1)S(1)} %broadcast_in_dim.44), kind=kLoop, calls=%fused_computation.10 | loop fusion | flops 1179648 | bytes 4719168 | tf_op jit(solution)/shard_map/jit(_where)/select_n | solution.py:29
  30.3 5.1 %all-to-all-start.1 = ((bf16[8,72,2048]{2,1,0:T(8,128)(2,1)}), bf16[8,72,2048]{2,1,0:T(8,128)(2,1)S(1)}, u32[]{:S(2)}, u32[]{:S(2)}) async-start(bf16[8,72,2048]{2,1,0:T(8,128)(2,1)} %broadcast_select_fusion), calls=%async_computation.1 | async-start | bytes 4718592 | tf_op jit(solution)/shard_map/all_to_all | solution.py:36
  35.5 54.5 %all-to-all-done.1 = bf16[8,72,2048]{2,1,0:T(8,128)(2,1)S(1)} async-done(((bf16[8,72,2048]{2,1,0:T(8,128)(2,1)}), bf16[8,72,2048]{2,1,0:T(8,128)(2,1)S(1)}, u32[]{:S(2)}, u32[]{:S(2)}) %all-to-all-start.1) | async-done | bytes 2359328 | tf_op jit(solution)/shard_map/all_to_all | solution.py:36
  90.1 5.5 %fusion.2 = bf16[768,2048]{0,1:T(8,128)(2,1)} fusion(bf16[576,768]{1,0:T(8,128)(2,1)} %param.8, bf16[576,2048]{1,0:T(8,128)(2,1)S(1)} %bitcast.16, f32[576]{0:T(1024)S(1)} %reshape.79), kind=kOutput, calls=%fused_computation.8 | convolution fusion | flops 1817051136 | bytes 6392064 | tf_op jit(solution)/shard_map/dot_general | solution.py:61
  95.6 4.7 %copy.26 = bf16[768,2048]{1,0:T(8,128)(2,1)} copy(bf16[768,2048]{0,1:T(8,128)(2,1)} %fusion.2) | data formatting | bytes 6291456
  100.3 5.1 %multiply_reduce_fusion = (f32[576]{0:T(1024)S(1)}, bf16[576,768]{1,0:T(8,128)(2,1)}) fusion(bf16[576,768]{1,0:T(8,128)(2,1)} %param.8, f32[576]{0:T(1024)S(1)} %reshape.79, bf16[576,2048]{1,0:T(8,128)(2,1)S(1)} %bitcast.17, bf16[1,768,2048]{2,1,0:T(8,128)(2,1)} %all-gather.3.cloned.1.call-done), kind=kOutput, calls=%fused_computation.11 | convolution fusion | flops 1814150656 | bytes 7279104 | tf_op jit(solution)/shard_map/dot_general | solution.py:57
  105.4 0.7 all_to_all.18
  106.1 3.3 %all-to-all-start.2 = ((f32[8,1,72]{2,1,0:T(1,128)}), f32[8,1,72]{2,1,0:T(1,128)S(1)}, u32[]{:S(2)}, u32[]{:S(2)}) async-start(f32[8,1,72]{2,1,0:T(1,128)} %all_to_all.18), calls=%async_computation.2 | async-start | bytes 8192 | tf_op jit(solution)/shard_map/all_to_all | solution.py:68
  109.4 5.4 %all-to-all-done.2 = f32[8,1,72]{2,1,0:T(1,128)S(1)} async-done(((f32[8,1,72]{2,1,0:T(1,128)}), f32[8,1,72]{2,1,0:T(1,128)S(1)}, u32[]{:S(2)}, u32[]{:S(2)}) %all-to-all-start.2) | async-done | bytes 2336 | tf_op jit(solution)/shard_map/all_to_all | solution.py:68
  114.8 0.5 broadcast.69
  115.3 0.7 reduce.9
  116.1 1.9 %gather_fusion.2 = f32[384]{0:T(512)S(1)} fusion(f32[576]{0:T(1024)S(1)} %reshape.77, s32[1024]{0:T(1024)S(1)} %pad_clamp_fusion), kind=kCustom, calls=%fused_computation.2 | custom fusion | bytes 4608 | tf_op jit(solution)/shard_map/gather | solution.py:71
  118.0 0.1 reshape.78
  118.1 0.7 copy.25
  118.8 24.6 %reduce-scatter.4.cloned.1.call-done = bf16[192,2048]{1,0:T(8,128)(2,1)} async-done(((bf16[768,2048]{1,0:T(8,128)(2,1)}), bf16[192,2048]{1,0:T(8,128)(2,1)}) %reduce-scatter.4.cloned.1.call-update) | async-done | bytes 786448
  143.3 2.2 %copy.27 = bf16[192,2048]{0,1:T(8,128)(2,1)} copy(bf16[192,2048]{1,0:T(8,128)(2,1)} %reduce-scatter.4.cloned.1.call-done) | data formatting | bytes 1572864
  145.6 1.4 bitcast_convert_fusion
  146.9 1.7 %copy.24 = f32[1,192,2048]{2,1,0:T(8,128)} copy(f32[1,192,2048]{1,2,0:T(8,128)S(1)} %bitcast_convert_fusion) | data formatting | bytes 3145728
  (19 shorter events, 0.4 us)
Async XLA Ops:
  7.2 18.0 %copy-start = (bf16[192,2048]{1,0:T(8,128)(2,1)S(1)}, bf16[192,2048]{1,0:T(8,128)(2,1)}, u32[]{:S(2)}) copy-start(bf16[192,2048]{1,0:T(8,128)(2,1)} %param.5) | copy-start | bytes 2359300
  18.0 12.3 %all-to-all-start = ((bf16[8,1,72]{2,1,0:T(2,128)(2,1)}), bf16[8,1,72]{2,1,0:T(2,128)(2,1)S(1)}, u32[]{:S(2)}, u32[]{:S(2)}) async-start(bf16[8,1,72]{2,1,0:T(2,128)(2,1)} %all_to_all.20), calls=%async_computation | async-start | bytes 8192 | tf_op jit(solution)/shard_map/all_to_all | solution.py:43
  24.3 76.0 %all-gather.3.cloned.1.call-start = ((), (), s32[]{:S(2)}) async-start(), calls=%async_computation.4 | async-start | bytes 3932160 | tf_op jit(solution)/shard_map/all_gather | solution.py:56
  30.3 59.8 %all-to-all-start.1 = ((bf16[8,72,2048]{2,1,0:T(8,128)(2,1)}), bf16[8,72,2048]{2,1,0:T(8,128)(2,1)S(1)}, u32[]{:S(2)}, u32[]{:S(2)}) async-start(bf16[8,72,2048]{2,1,0:T(8,128)(2,1)} %broadcast_select_fusion), calls=%async_computation.1 | async-start | bytes 4718592 | tf_op jit(solution)/shard_map/all_to_all | solution.py:36
  35.4 108.0 %reduce-scatter.4.cloned.1.call-start = ((), (), s32[]{:S(2)}) async-start(), calls=%async_computation.5 | async-start | bytes 3932160
  106.1 8.7 %all-to-all-start.2 = ((f32[8,1,72]{2,1,0:T(1,128)}), f32[8,1,72]{2,1,0:T(1,128)S(1)}, u32[]{:S(2)}, u32[]{:S(2)}) async-start(f32[8,1,72]{2,1,0:T(1,128)} %all_to_all.18), calls=%async_computation.2 | async-start | bytes 8192 | tf_op jit(solution)/shard_map/all_to_all | solution.py:68
Sparse Core Ops, SparseCore 0:
  27.0 45.4 all-gather.2
  100.4 42.8 reduce-scatter.3
where the time goes:
time: 156 us; the launch traced here: 155 us
  waiting for transfers between devices  85.2 us (55%)
  local copies, waits for them, and re-layouts  25.9 us (17%)
  starting transfers between devices  14.8 us (9%)
  between operations  14.2 us (9%)
  matrix products  10.6 us (7%)
  other arithmetic  4.73 us (3%)
    all_to_all x1, waiting for transfers between devices, per_device(): lax.all_to_all(send_rows.reshape(experts, capacity, features), 'expert',...  54.5 us
    unnamed x3, waiting for transfers between devices  25.3 us
    unnamed x8, local copies, waits for them, and re-layouts  11 us
    all_to_all x1, starting transfers between devices, per_device(): lax.all_to_all(send_weights.reshape(experts, capacity), 'expert', split_a...  6.33 us
    dot_general x1, matrix products, per_device(): lax.dot_general(saved_hidden, weighted, (((0,), (0,)), ((), ())), preferr...  5.51 us
    all_to_all x1, waiting for transfers between devices, per_device(): lax.all_to_all(route_terms.reshape(experts, capacity), 'expert', split_ax...  5.4 us
    all_to_all x1, starting transfers between devices, per_device(): lax.all_to_all(send_rows.reshape(experts, capacity, features), 'expert',...  5.09 us
    dot_general x1, matrix products, per_device(): lax.dot_general(grad_rows, full_weight, contract, preferred_element_type=...  5.08 us
  transfers between devices with their start and end apart: 5, of which 3 were waited for; matrix products, arithmetic and copies ran while one was open for 16% of the time, Pallas kernels for 0%

commit v1 on v0

--- a/solution.py
+++ b/solution.py
@@ -2,6 +2,24 @@
 import jax.numpy as jnp
 from jax import lax
 from jax.sharding import PartitionSpec as P
+
+
+def open_axis_part(message, dim_at, unit):
+    tile_out = message.shape
+    r1 = message.reshape(
+        *tile_out[:dim_at], unit, tile_out[dim_at] // unit, *tile_out[dim_at + 1 :]
+    )
+    carry_out = jnp.moveaxis(r1, dim_at, 0)
+    return carry_out
+
+
+def use_column(xs, k_dim):
+    xs = jnp.moveaxis(xs, 0, k_dim)
+    finding = xs.shape
+    u_next = xs.reshape(
+        *finding[:k_dim], finding[k_dim] * finding[k_dim + 1], *finding[k_dim + 2 :]
+    )
+    return u_next
 
 
 def route_slots(routes, experts, capacity):
@@ -32,14 +50,24 @@
     send_weights = jnp.where(
         is_live, combine_weights.reshape(-1)[safe_index], jnp.zeros((), jnp.bfloat16)
     )
+
+    def rounds_list(mine, along_axis, x_local, frame):
+        opened = lax.psum(1, axis_name=along_axis)
+        v_now = lax.axis_index(along_axis)
+        heard, newest = (opened, v_now)
+        parts_out = open_axis_part(mine, x_local, heard)
+        local_part = parts_out
+        for ix in range(1, heard):
+            o_now, field_out = ((newest + ix) % heard, (newest - ix) % heard)
+            earlier = lax.dynamic_index_in_dim(parts_out, o_now, 0)
+            reply = tuple(((q, (q + ix) % heard) for q in range(heard)))
+            now = lax.ppermute(earlier, axis_name=along_axis, perm=reply)
+            local_part = lax.dynamic_update_slice_in_dim(local_part, now, field_out, axis=0)
+        then = use_column(local_part, frame)
+        return then
+
     recv_rows, recv_weights = (
-        lax.all_to_all(
-            send_rows.reshape(experts, capacity, features),
-            "expert",
-            split_axis=0,
-            concat_axis=0,
-            tiled=True,
-        ),
+        rounds_list(send_rows.reshape(experts, capacity, features), "expert", 0, 0),
         lax.all_to_all(
             send_weights.reshape(experts, capacity),
             "expert",

time: 156 us -> 147 us (0.942)
  waiting for transfers between devices: 85.2 us -> 59.6 us
  starting transfers between devices: 14.8 us -> 29.2 us
  local copies, waits for them, and re-layouts: 25.9 us -> 30.8 us
    all_to_all x1 -> x0, waiting for transfers between devices: 54.5 us -> none  [per_device(): lax.all_to_all(send_rows.reshape(experts, capacity, features), 'expert',...]
    ppermute x0 -> x7, waiting for transfers between devices: none -> 23.7 us  [rounds_list(): now = lax.ppermute(earlier, axis_name=along_axis, perm=reply)]
    all_to_all x1, starting transfers between devices: 3.31 us -> 17.7 us  [per_device(): lax.all_to_all(route_terms.reshape(experts, capacity), 'expert', split_ax...]
    ppermute x0 -> x7, starting transfers between devices: none -> 6.59 us  [rounds_list(): now = lax.ppermute(earlier, axis_name=along_axis, perm=reply)]
    all_to_all x1 -> x0, starting transfers between devices: 5.09 us -> none  [per_device(): lax.all_to_all(send_rows.reshape(experts, capacity, features), 'expert',...]
    all_to_all x1, waiting for transfers between devices: 0.01 us -> 3.89 us  [per_device(): lax.all_to_all(send_weights.reshape(experts, capacity), 'expert', split_a...]
    dynamic_slice x0 -> x2, local copies, waits for them, and re-layouts: none -> 2.11 us  [rounds_list(): earlier = lax.dynamic_index_in_dim(parts_out, o_now, 0)]
    dynamic_update_slice x0 -> x6, local copies, waits for them, and re-layouts: none -> 2.06 us  [rounds_list(): lax.dynamic_update_slice_in_dim(local_part, now, field_out, axis=0)]
  transfers between devices with their start and end apart: 5 -> 11, of which waited for: 3 -> 7; matrix products, arithmetic and copies ran while one was open for 16% -> 24% of each run, Pallas kernels for 0% -> 0%
where the time goes in v1:
time: 147 us
  waiting for transfers between devices  59.6 us (41%)
  local copies, waits for them, and re-layouts  30.8 us (21%)
  starting transfers between devices  29.2 us (20%)
  between operations  14.5 us (10%)
  matrix products  9.48 us (6%)
  other arithmetic  3.28 us (2%)
    unnamed x3, waiting for transfers between devices  26.5 us
    ppermute x7, waiting for transfers between devices, rounds_list(): now = lax.ppermute(earlier, axis_name=along_axis, perm=reply)  23.7 us
    all_to_all x1, starting transfers between devices, per_device(): lax.all_to_all(route_terms.reshape(experts, capacity), 'expert', split_ax...  17.7 us
    unnamed x16, local copies, waits for them, and re-layouts  11.7 us
    ppermute x7, starting transfers between devices, rounds_list(): now = lax.ppermute(earlier, axis_name=along_axis, perm=reply)  6.59 us
    all_to_all x1, waiting for transfers between devices, per_device(): lax.all_to_all(route_terms.reshape(experts, capacity), 'expert', split_ax...  5.47 us
    dot_general x1, matrix products, per_device(): lax.dot_general(grad_rows, full_weight, contract, preferred_element_type=...  5.08 us
    all_to_all x1, starting transfers between devices, per_device(): lax.all_to_all(send_weights.reshape(experts, capacity), 'expert', split_a...  4.83 us
  transfers between devices with their start and end apart: 11, of which 7 were waited for; matrix products, arithmetic and copies ran while one was open for 24% of the time, Pallas kernels for 0%

profile of v1, /device:TPU:0, one launch (start us, length us, event | category | flops | bytes accessed | tf_op | source)
XLA Modules:
  0.0 146.8 jit_solution(18272878021030348113)
XLA Ops:
  7.2 0.7 all-gather.3.cloned.1.call-update
  7.9 0.8 copy.21
  8.7 0.7 broadcast_multiply_fusion
  10.1 2.9 %scatter_custom_fusion = s32[576]{0:T(1024)S(1)} fusion(s32[384]{0:T(512)S(1)} %fusion.9, s32[384]{0:T(512)S(1)} %iota.10, s32[]{:T(128)} %constant.114.clone.1), kind=kCustom, calls=%fused_computation.46 | custom fusion | bytes 2308 | tf_op jit(solution)/shard_map/scatter | solution.py:43
  13.2 3.4 %gather_fusion.1 = bf16[576,2048]{1,0:T(8,128)(2,1)S(1)} fusion(bf16[192,2048]{1,0:T(8,128)(2,1)S(1)} %copy-done, s32[1024]{0:T(1024)S(1)} %pad_clamp_fusion.1), kind=kCustom, calls=%fused_computation.1 | custom fusion | bytes 4720896 | tf_op jit(solution)/shard_map/gather | solution.py:48
  16.9 1.4 copy-done.1
  19.2 3.9 %gather_fusion = bf16[576]{0:T(1024)(128)(2,1)S(1)} fusion(bf16[384]{0:T(512)(128)(2,1)S(1)} %reshape.82, s32[1024]{0:T(1024)S(1)} %pad_clamp_fusion.2), kind=kCustom, calls=%fused_computation | custom fusion | bytes 4608 | tf_op jit(solution)/shard_map/gather | solution.py:51
  23.2 4.2 %collective-permute-done = bf16[1,1,72,2048]{3,2,0,1:T(8,128)(2,1)} collective-permute-done((bf16[1,1,72,2048]{3,2,0,1:T(8,128)(2,1)S(1)}, bf16[1,1,72,2048]{3,2,0,1:T(8,128)(2,1)}, u32[]{:S(2)}, u32[]{:S(2)}) %collective-permute-start) | collective-permute-done | bytes 294944 | tf_op jit(solution)/shard_map/ppermute | solution.py:64
  27.4 2.1 %constant_dynamic-slice_fusion = (bf16[1,1,72,2048]{3,2,0,1:T(8,128)(2,1)S(1)}, bf16[1,1,72,2048]{3,2,0,1:T(8,128)(2,1)}, bf16[1,1,72,2048]{3,2,0,1:T(8,128)(2,1...) fusion(bf16[8,1,72,2048]{3,2,0,1:T(8,128)(2,1)S(1)} %copy-done., ...), kind=kLoop, calls=%fused_computation.32 | loop fusion | bytes 4128796 | tf_op jit(solution)/shard_map/jit(dynamic_index_in_dim)/dynamic_slice | solution.py:62
  29.8 0.7 all_to_all.16
  30.4 4.8 %all-to-all-start = ((bf16[8,1,72]{2,1,0:T(2,128)(2,1)}), bf16[8,1,72]{2,1,0:T(2,128)(2,1)S(1)}, u32[]{:S(2)}, u32[]{:S(2)}) async-start(bf16[8,1,72]{2,1,0:T(2,128)(2,1)} %all_to_all.16), calls=%async_computation | async-start | bytes 8192 | tf_op jit(solution)/shard_map/all_to_all | solution.py:71
  35.4 1.6 %collective-permute-start.2 = (bf16[1,1,72,2048]{3,2,0,1:T(8,128)(2,1)}, bf16[1,1,72,2048]{3,2,0,1:T(8,128)(2,1)}, u32[]{:S(2)}, u32[]{:S(2)}) collective-permute-start(bf16[1,1,72,2048]{3,2,0,1:T(8,128)(2,1)} %get-tuple-element.21), channel_id=1, source_target_pairs={{0,3},{1,4},{2,5},{3,6},{4,7},{5,0},{6,1},{7,2},{8,11},{9,12},{10,... | collective-permute-start | bytes 884744 | tf_op jit(solution)/shard_map/ppermute | solution.py:64
  37.0 3.9 %all-to-all-done = bf16[8,1,72]{2,1,0:T(2,128)(2,1)S(1)} async-done(((bf16[8,1,72]{2,1,0:T(2,128)(2,1)}), bf16[8,1,72]{2,1,0:T(2,128)(2,1)S(1)}, u32[]{:S(2)}, u32[]{:S(2)}) %all-to-all-start) | async-done | bytes 1184 | tf_op jit(solution)/shard_map/all_to_all | solution.py:71
  41.6 1.6 %collective-permute-start.4 = (bf16[1,1,72,2048]{3,2,0,1:T(8,128)(2,1)}, bf16[1,1,72,2048]{3,2,0,1:T(8,128)(2,1)S(1)}, u32[]{:S(2)}, u32[]{:S(2)}) collective-permute-start(bf16[1,1,72,2048]{3,2,0,1:T(8,128)(2,1)} %get-tuple-element.19), channel_id=1, source_target_pairs={{0,5},{1,6},{2,7},{3,0},{4,1},{5,2},{6,3},{7,4},{8,13},{9,14},{10,... | collective-permute-start | bytes 884744 | tf_op jit(solution)/shard_map/ppermute | solution.py:64
  43.2 0.9 collective-permute-start.5
  44.1 1.2 collective-permute-start.6
  45.2 1.0 constant_dynamic-update-slice_fusion.5
  46.2 14.4 %collective-permute-done.2 = bf16[1,1,72,2048]{3,2,0,1:T(8,128)(2,1)} collective-permute-done((bf16[1,1,72,2048]{3,2,0,1:T(8,128)(2,1)}, bf16[1,1,72,2048]{3,2,0,1:T(8,128)(2,1)}, u32[]{:S(2)}, u32[]{:S(2)}) %collective-permute-start.2) | collective-permute-done | bytes 294944 | tf_op jit(solution)/shard_map/ppermute | solution.py:64
  60.6 1.0 constant_dynamic-update-slice_fusion.4
  61.6 1.6 %collective-permute-done.3 = bf16[1,1,72,2048]{3,2,0,1:T(8,128)(2,1)S(1)} collective-permute-done((bf16[1,1,72,2048]{3,2,0,1:T(8,128)(2,1)}, bf16[1,1,72,2048]{3,2,0,1:T(8,128)(2,1)S(1)}, u32[]{:S(2)}, u32[]{:S(2)}) %collective-permute-start.3) | collective-permute-done | bytes 294944 | tf_op jit(solution)/shard_map/ppermute | solution.py:64
  63.4 3.4 %collective-permute-done.6 = bf16[1,1,72,2048]{3,2,0,1:T(8,128)(2,1)S(1)} collective-permute-done((bf16[1,1,72,2048]{3,2,0,1:T(8,128)(2,1)S(1)}, bf16[1,1,72,2048]{3,2,0,1:T(8,128)(2,1)S(1)}, u32[]{:S(2)}, u32[]{:S(2)}) %collective-permute-start.6) | collective-permute-done | bytes 294944 | tf_op jit(solution)/shard_map/ppermute | solution.py:64
  66.8 4.4 %fusion.2 = bf16[768,2048]{0,1:T(8,128)(2,1)} fusion(bf16[576,768]{1,0:T(8,128)(2,1)S(1)} %copy-done.4, bf16[576,2048]{1,0:T(8,128)(2,1)S(1)} %bitcast.16, f32[576]{0:T(1024)S(1)} %reshape.85), kind=kOutput, calls=%fused_computation.8 | convolution fusion | flops 1817051136 | bytes 6392064 | tf_op jit(solution)/shard_map/dot_general | solution.py:89
  71.2 4.7 %copy.26 = bf16[768,2048]{1,0:T(8,128)(2,1)} copy(bf16[768,2048]{0,1:T(8,128)(2,1)} %fusion.2) | data formatting | bytes 6291456
  76.0 5.1 %multiply_reduce_fusion = (f32[576]{0:T(1024)S(1)}, bf16[576,768]{1,0:T(8,128)(2,1)}) fusion(bf16[576,768]{1,0:T(8,128)(2,1)} %param.8, f32[576]{0:T(1024)S(1)} %reshape.85, bf16[576,2048]{1,0:T(8,128)(2,1)S(1)} %bitcast.17, bf16[1,768,2048]{2,1,0:T(8,128)(2,1)} %all-gather.3.cloned.1.call-done), kind=kOutput, calls=%fused_computation.11 | convolution fusion | flops 1814150656 | bytes 7279104 | tf_op jit(solution)/shard_map/dot_general | solution.py:85
  81.1 0.7 all_to_all.14
  81.7 17.7 %all-to-all-start.1 = ((f32[8,1,72]{2,1,0:T(1,128)}), f32[8,1,72]{2,1,0:T(1,128)S(1)}, u32[]{:S(2)}, u32[]{:S(2)}) async-start(f32[8,1,72]{2,1,0:T(1,128)} %all_to_all.14), calls=%async_computation.1 | async-start | bytes 8192 | tf_op jit(solution)/shard_map/all_to_all | solution.py:96
  99.5 5.5 %all-to-all-done.1 = f32[8,1,72]{2,1,0:T(1,128)S(1)} async-done(((f32[8,1,72]{2,1,0:T(1,128)}), f32[8,1,72]{2,1,0:T(1,128)S(1)}, u32[]{:S(2)}, u32[]{:S(2)}) %all-to-all-start.1) | async-done | bytes 2336 | tf_op jit(solution)/shard_map/all_to_all | solution.py:96
  106.2 1.9 %gather_fusion.2 = f32[384]{0:T(512)S(1)} fusion(f32[576]{0:T(1024)S(1)} %reshape.83, s32[1024]{0:T(1024)S(1)} %pad_clamp_fusion), kind=kCustom, calls=%fused_computation.2 | custom fusion | bytes 4608 | tf_op jit(solution)/shard_map/gather | solution.py:99
  108.9 25.8 %reduce-scatter.4.cloned.1.call-done = bf16[192,2048]{1,0:T(8,128)(2,1)} async-done(((bf16[768,2048]{1,0:T(8,128)(2,1)}), bf16[192,2048]{1,0:T(8,128)(2,1)}) %reduce-scatter.4.cloned.1.call-update) | async-done | bytes 786448
  134.7 2.2 %copy.27 = bf16[192,2048]{0,1:T(8,128)(2,1)} copy(bf16[192,2048]{1,0:T(8,128)(2,1)} %reduce-scatter.4.cloned.1.call-done) | data formatting | bytes 1572864
  136.9 1.4 bitcast_convert_fusion
  138.3 1.7 %copy.24 = f32[1,192,2048]{2,1,0:T(8,128)} copy(f32[1,192,2048]{1,2,0:T(8,128)S(1)} %bitcast_convert_fusion) | data formatting | bytes 3145728
  (47 shorter events, 5.0 us)
Async XLA Ops:
  7.2 6.0 %copy-start = (bf16[192,2048]{1,0:T(8,128)(2,1)S(1)}, bf16[192,2048]{1,0:T(8,128)(2,1)}, u32[]{:S(2)}) copy-start(bf16[192,2048]{1,0:T(8,128)(2,1)} %param.5) | copy-start | bytes 2359300
  7.2 68.8 %all-gather.3.cloned.1.call-start = ((), (), s32[]{:S(2)}) async-start(), calls=%async_computation.3 | async-start | bytes 3932160 | tf_op jit(solution)/shard_map/all_gather | solution.py:84
  16.6 2.2 %copy-start.3 = (bf16[192,2]{0,1:T(2,128)(2,1)S(1)}, bf16[192,2]{0,1:T(2,128)(2,1)}, u32[]{:S(2)}) copy-start(bf16[192,2]{0,1:T(2,128)(2,1)} %param.7) | copy-start | bytes 2308
  16.9 1.5 copy-start.1
  18.3 9.1 %copy-start.2 = (bf16[8,1,72,2048]{3,2,0,1:T(8,128)(2,1)S(1)}, bf16[8,1,72,2048]{3,2,0,1:T(8,128)(2,1)}, u32[]{:S(2)}) copy-start(bf16[8,1,72,2048]{3,2,0,1:T(8,128)(2,1)} %copy-done.1) | copy-start | bytes 7077892
  18.3 9.1 %collective-permute-start = (bf16[1,1,72,2048]{3,2,0,1:T(8,128)(2,1)S(1)}, bf16[1,1,72,2048]{3,2,0,1:T(8,128)(2,1)}, u32[]{:S(2)}, u32[]{:S(2)}) collective-permute-start(bf16[1,1,72,2048]{3,2,0,1:T(8,128)(2,1)S(1)} %constant_dynamic-slice_fusion.6), channel_id=1, source_target_pairs={{0,1},{1,2},{2,3},{3,4},{4,5},{5,6},{6,7},{7,0},{8,9},{9,10},{10,1... | collective-permute-start | bytes 884744 | tf_op jit(solution)/shard_map/ppermute | solution.py:64
  29.5 14.6 %collective-permute-start.1 = (bf16[1,1,72,2048]{3,2,0,1:T(8,128)(2,1)}, bf16[1,1,72,2048]{3,2,0,1:T(8,128)(2,1)}, u32[]{:S(2)}, u32[]{:S(2)}) collective-permute-start(bf16[1,1,72,2048]{3,2,0,1:T(8,128)(2,1)} %get-tuple-element.22), channel_id=1, source_target_pairs={{0,2},{1,3},{2,4},{3,5},{4,6},{5,7},{6,0},{7,1},{8,10},{9,11},{10,... | collective-permute-start | bytes 884744 | tf_op jit(solution)/shard_map/ppermute | solution.py:64
  30.4 10.5 %all-to-all-start = ((bf16[8,1,72]{2,1,0:T(2,128)(2,1)}), bf16[8,1,72]{2,1,0:T(2,128)(2,1)S(1)}, u32[]{:S(2)}, u32[]{:S(2)}) async-start(bf16[8,1,72]{2,1,0:T(2,128)(2,1)} %all_to_all.16), calls=%async_computation | async-start | bytes 8192 | tf_op jit(solution)/shard_map/all_to_all | solution.py:71
  35.3 99.4 %reduce-scatter.4.cloned.1.call-start = ((), (), s32[]{:S(2)}) async-start(), calls=%async_computation.4 | async-start | bytes 3932160
  35.4 25.2 %collective-permute-start.2 = (bf16[1,1,72,2048]{3,2,0,1:T(8,128)(2,1)}, bf16[1,1,72,2048]{3,2,0,1:T(8,128)(2,1)}, u32[]{:S(2)}, u32[]{:S(2)}) collective-permute-start(bf16[1,1,72,2048]{3,2,0,1:T(8,128)(2,1)} %get-tuple-element.21), channel_id=1, source_target_pairs={{0,3},{1,4},{2,5},{3,6},{4,7},{5,0},{6,1},{7,2},{8,11},{9,12},{10,... | collective-permute-start | bytes 884744 | tf_op jit(solution)/shard_map/ppermute | solution.py:64
  41.0 25.8 %copy-start.4 = (bf16[576,768]{1,0:T(8,128)(2,1)S(1)}, bf16[576,768]{1,0:T(8,128)(2,1)}, u32[]{:S(2)}) copy-start(bf16[576,768]{1,0:T(8,128)(2,1)} %param.8) | copy-start | bytes 2654212
  41.0 22.2 %collective-permute-start.3 = (bf16[1,1,72,2048]{3,2,0,1:T(8,128)(2,1)}, bf16[1,1,72,2048]{3,2,0,1:T(8,128)(2,1)S(1)}, u32[]{:S(2)}, u32[]{:S(2)}) collective-permute-start(bf16[1,1,72,2048]{3,2,0,1:T(8,128)(2,1)} %get-tuple-element.20), channel_id=1, source_target_pairs={{0,4},{1,5},{2,6},{3,7},{4,0},{5,1},{6,2},{7,3},{8,12},{9,13},{10,... | collective-permute-start | bytes 884744 | tf_op jit(solution)/shard_map/ppermute | solution.py:64
  41.6 21.7 %collective-permute-start.4 = (bf16[1,1,72,2048]{3,2,0,1:T(8,128)(2,1)}, bf16[1,1,72,2048]{3,2,0,1:T(8,128)(2,1)S(1)}, u32[]{:S(2)}, u32[]{:S(2)}) collective-permute-start(bf16[1,1,72,2048]{3,2,0,1:T(8,128)(2,1)} %get-tuple-element.19), channel_id=1, source_target_pairs={{0,5},{1,6},{2,7},{3,0},{4,1},{5,2},{6,3},{7,4},{8,13},{9,14},{10,... | collective-permute-start | bytes 884744 | tf_op jit(solution)/shard_map/ppermute | solution.py:64
  43.2 20.2 %collective-permute-start.5 = (bf16[1,1,72,2048]{3,2,0,1:T(8,128)(2,1)}, bf16[1,1,72,2048]{3,2,0,1:T(8,128)(2,1)S(1)}, u32[]{:S(2)}, u32[]{:S(2)}) collective-permute-start(bf16[1,1,72,2048]{3,2,0,1:T(8,128)(2,1)} %get-tuple-element.18), channel_id=1, source_target_pairs={{0,6},{1,7},{2,0},{3,1},{4,2},{5,3},{6,4},{7,5},{8,14},{9,15},{10,... | collective-permute-start | bytes 884744 | tf_op jit(solution)/shard_map/ppermute | solution.py:64
  44.1 22.7 %collective-permute-start.6 = (bf16[1,1,72,2048]{3,2,0,1:T(8,128)(2,1)S(1)}, bf16[1,1,72,2048]{3,2,0,1:T(8,128)(2,1)S(1)}, u32[]{:S(2)}, u32[]{:S(2)}) collective-permute-start(bf16[1,1,72,2048]{3,2,0,1:T(8,128)(2,1)S(1)} %get-tuple-element.17), channel_id=1, source_target_pairs={{0,7},{1,0},{2,1},{3,2},{4,3},{5,4},{6,5},{7,6},{8,15},{9,8},{10,9... | collective-permute-start | bytes 884744 | tf_op jit(solution)/shard_map/ppermute | solution.py:64
  81.7 23.2 %all-to-all-start.1 = ((f32[8,1,72]{2,1,0:T(1,128)}), f32[8,1,72]{2,1,0:T(1,128)S(1)}, u32[]{:S(2)}, u32[]{:S(2)}) async-start(f32[8,1,72]{2,1,0:T(1,128)} %all_to_all.14), calls=%async_computation.1 | async-start | bytes 8192 | tf_op jit(solution)/shard_map/all_to_all | solution.py:96
Sparse Core Ops, SparseCore 0:
  9.9 46.6 all-gather.2
  76.1 58.5 reduce-scatter.3
